TPU v7x, 256 devices: a whole 4x4x8 slice. The times are simulated.
256 devices in a mesh: group: 32 (over x, z_hi, core), head: 8 (over z_lo, y).
Axes of the slice: x: 4, y: 4, z: 8 (z_hi: 4, z_lo: 2; z = z_hi * 2 + z_lo), core: 2. Of those that a mesh axis runs over, the one named last changes fastest.
Arguments:
- query: bfloat16 [32, 512, 5120], P('group', None, 'head'), may hold values from -1.7265625 to 1.7265625
- key: bfloat16 [32, 512, 5120], P('group', None, 'head'), may hold values from -1.7265625 to 1.7265625
- value: bfloat16 [32, 512, 5120], P('group', None, 'head'), may hold values from -6 to 6
- output: bfloat16 [32, 512, 5120], P('group', None, 'head'), may hold values from -1.5 to 1.5
- grad_out: bfloat16 [32, 512, 5120], P('group', 'head'), may hold values from -169 to 169
- log_sum: float32 [32, 40, 512], P('group', 'head'), as said below
- group_length: int32 [32], replicated, may hold values from 256 to 512, as said below
- cache_source: int32 [32], replicated, may hold values from -1 to 30, as said below
Outputs:
- grad_query: bfloat16 [32, 512, 5120], P('group', 'head')
- grad_key: bfloat16 [32, 512, 5120], P('group', 'head')
- grad_value: bfloat16 [32, 512, 5120], P('group', 'head')
Inputs may be any that keep to these rules, and one draw needn't show every extreme that they name: group_length[c] counts the first, live token slots of group c; some group is full. cache_source[c] is c - 1 where group c attends the preceding group's cache and -1 where a rollout starts; it is -1 for group 0 and c - 1 for the last group. `log_sum`: each entry lies between ln(512) + 0.2 and ln(1024) + 0.8.
All inputs are finite; a program needn't handle non-finite values.
Results may differ from a plain program's by a relative error of at most 0.0049.
Values may be sent and summed in bfloat16 or wider, within the bound.
A program may use at most 128 MiB of HBM per device.

v0:
```python
import functools
import math

import jax
import jax.numpy as jnp
from jax import lax
from jax.experimental import pallas as pl
from jax.experimental.pallas import tpu as pltpu
from jax.sharding import PartitionSpec as P

HEAD_DIM = 128
MESH = pl.DeviceIdType.MESH
SCALE = HEAD_DIM**-0.5
LOG2E = math.log2(math.e)
DEAD = 1e30


def dot_nt(a, b):
    return lax.dot_general(a, b, (((1,), (1,)), ((), ())), preferred_element_type=jnp.float32)


def dot_nn(a, b):
    return jnp.dot(a, b, preferred_element_type=jnp.float32)


def block_grads(q, g, lse_row, delta_row, k, kt, v):
    prob = jnp.exp2(dot_nt(k, q) * (SCALE * LOG2E) - lse_row)
    grad_score = (prob * (dot_nt(v, g) - delta_row)).astype(jnp.bfloat16)
    grad_v = dot_nn(prob.astype(jnp.bfloat16), g)
    grad_k = dot_nn(grad_score, q)
    grad_q = dot_nn(kt, grad_score).T
    return grad_q, grad_k, grad_v


def kernel(
    len_ref, source_ref, q_hbm, k_hbm, v_hbm, o_hbm, g_hbm, lse_ref,
    out_q, out_k, out_v,
    q_own, k_own, v_own, o_own, g_own, q_next, g_next, lse_next, delta_own, delta_next,
    acc_q, acc_k, acc_v, stage, cross_q, cross_in,
    load_sem, local_sem, g_send, g_recv, lse_sem, q_sem, fwd_sem, delta_sem, cross_sem,
    out_send, out_recv, out_local,
):
    heads, length, _ = q_own.shape
    groups = lax.axis_size("group")
    parts = lax.axis_size("head")
    rows = length // parts
    group, me = lax.axis_index("group"), lax.axis_index("head")
    after, before = lax.rem(group + 1, groups), lax.rem(group + groups - 1, groups)

    def lanes(i):
        return pl.ds(pl.multiple_of(i * HEAD_DIM, HEAD_DIM), HEAD_DIM)

    def token_rows(part):
        return pl.ds(pl.multiple_of(part * rows, rows), rows)

    def to(src, dst, sems, slot, device):
        return pltpu.make_async_remote_copy(
            src_ref=src, dst_ref=dst, send_sem=sems.at[0, slot], recv_sem=sems.at[1, slot],
            device_id=device, device_id_type=MESH,
        )

    def loads(i):
        pairs = ((k_hbm, k_own), (v_hbm, v_own), (q_hbm, q_own), (o_hbm, o_own))
        return [
            pltpu.make_async_copy(src.at[0, :, lanes(i)], dst.at[i], load_sem.at[at, i])
            for at, (src, dst) in enumerate(pairs)
        ]

    def local_g(i):
        return pltpu.make_async_copy(
            g_hbm.at[0, :, lanes(me * heads + i)], g_own.at[i, token_rows(me)], local_sem.at[i]
        )

    def q_copy(i):
        return to(q_hbm.at[0, :, lanes(i)], q_next.at[i], q_sem, i, (before, me))

    def g_copy(i):
        return to(g_own.at[i], g_next.at[i], fwd_sem, i, (before, me))

    def delta_copy(i):
        return to(delta_own.at[i], delta_next.at[i], delta_sem, i, (before, me))

    def cross_copy(i):
        return to(cross_q.at[i], cross_in.at[i], cross_sem, i, (after, me))

    lse_copy = to(lse_ref.at[0], lse_next, lse_sem, 0, (before, me))

    barrier = pltpu.get_barrier_semaphore()

    @pl.loop(1, parts)
    def _(step):
        pl.semaphore_signal(
            barrier, inc=1, device_id=(group, lax.rem(me + step, parts)), device_id_type=MESH
        )

    for neighbour in (before, after):
        pl.semaphore_signal(barrier, inc=1, device_id=(neighbour, me), device_id_type=MESH)

    @pl.loop(0, heads)
    def _(i):
        local_g(i).start()
        for copy in loads(i):
            copy.start()

    pl.semaphore_wait(barrier, parts + 1)

    @pl.loop(0, heads)
    def _(i):
        @pl.loop(1, parts)
        def _(step):
            peer = lax.rem(me + step, parts)
            pltpu.make_async_remote_copy(
                src_ref=g_hbm.at[0, :, lanes(peer * heads + i)],
                dst_ref=g_own.at[i, token_rows(me)],
                send_sem=g_send, recv_sem=g_recv.at[i],
                device_id=(group, peer), device_id_type=MESH,
            ).start()

        q_copy(i).start()

    lse_copy.start()

    own_len = len_ref[group]
    after_len = jnp.where(source_ref[after] == group, len_ref[after], 0)
    query_at = lax.broadcasted_iota(jnp.int32, (1, length), 1)
    key_live = lax.broadcasted_iota(jnp.int32, (length, HEAD_DIM), 0) < own_len
    zero = jnp.zeros((), jnp.bfloat16)

    @pl.loop(0, heads)
    def _(i):
        others = g_own.at[i, pl.ds(0, (parts - 1) * rows)]
        pltpu.make_async_copy(others, others, g_recv.at[i]).wait()
        local_g(i).wait()
        g_copy(i).start()
        for copy in loads(i):
            copy.wait()
        g = g_own[i]
        product = g.astype(jnp.float32) * o_own[i].astype(jnp.float32)
        delta = jnp.sum(product.T, axis=0, keepdims=True)
        delta_own[i] = delta
        delta_copy(i).start()
        lse_row = jnp.where(query_at < own_len, lse_ref[0, pl.ds(i, 1), :] * LOG2E, DEAD)
        k = jnp.where(key_live, k_own[i], zero)
        grad_q, grad_k, grad_v = block_grads(q_own[i], g, lse_row, delta, k, k.T, v_own[i])
        acc_q[i] = grad_q
        acc_k[i] = grad_k
        acc_v[i] = grad_v

    lse_copy.wait_recv()

    def send_out(which, out, i):
        columns = lanes(me * heads + i)

        @pl.loop(1, parts)
        def _(step):
            peer = lax.rem(me + step, parts)
            pltpu.make_async_remote_copy(
                src_ref=stage.at[which, i, token_rows(peer)],
                dst_ref=out.at[0, :, columns],
                send_sem=out_send.at[which], recv_sem=out_recv.at[which],
                device_id=(group, peer), device_id_type=MESH,
            ).start()

        pltpu.make_async_copy(
            stage.at[which, i, token_rows(me)], out.at[0, :, columns], out_local.at[which]
        ).start()

    def finish_query(i):
        cross_copy(i).wait_recv()
        total = (acc_q[i] + cross_in[i].astype(jnp.float32)) * SCALE
        stage[0, i] = total.astype(jnp.bfloat16)
        send_out(0, out_q, i)

    @pl.loop(0, heads)
    def _(i):
        q_copy(i).wait_recv()
        g_copy(i).wait_recv()
        delta_copy(i).wait_recv()
        lse_row = jnp.where(query_at < after_len, lse_next[pl.ds(i, 1), :] * LOG2E, DEAD)
        k = jnp.where(key_live, k_own[i], zero)
        grad_q, grad_k, grad_v = block_grads(
            q_next[i], g_next[i], lse_row, delta_next[i], k, k.T, v_own[i]
        )
        cross_q[i] = grad_q.astype(jnp.bfloat16)
        cross_copy(i).start()
        sum_k = jnp.where(key_live, (acc_k[i] + grad_k) * SCALE, 0.0)
        stage[1, i] = sum_k.astype(jnp.bfloat16)
        send_out(1, out_k, i)
        sum_v = jnp.where(key_live, acc_v[i] + grad_v, 0.0)
        stage[2, i] = sum_v.astype(jnp.bfloat16)
        send_out(2, out_v, i)

        @pl.when(i > 0)
        def _():
            finish_query(i - 1)

    finish_query(heads - 1)

    for which, out in enumerate((out_q, out_k, out_v)):
        theirs = out.at[0, :, pl.ds(0, (parts - 1) * heads * HEAD_DIM)]
        mine = out.at[0, :, pl.ds(0, heads * HEAD_DIM)]
        pltpu.make_async_copy(theirs, theirs, out_recv.at[which]).wait()
        pltpu.make_async_copy(theirs, theirs, out_send.at[which]).wait()
        pltpu.make_async_copy(mine, mine, out_local.at[which]).wait()
    sent = g_hbm.at[0, :, pl.ds(0, (parts - 1) * heads * HEAD_DIM)]
    pltpu.make_async_copy(sent, sent, g_send).wait()
    lse_copy.wait_send()

    @pl.loop(0, heads)
    def _(i):
        q_copy(i).wait_send()
        g_copy(i).wait_send()
        delta_copy(i).wait_send()
        cross_copy(i).wait_send()


def on_device(query, key, value, output, grad_out, log_sum, group_length, cache_source):
    _, length, features = query.shape
    heads = features // HEAD_DIM
    per_head = (heads, length, HEAD_DIM)
    half = pltpu.VMEM(per_head, jnp.bfloat16)
    wide = pltpu.VMEM(per_head, jnp.float32)
    row = pltpu.VMEM((heads, 1, length), jnp.float32)
    dma = pltpu.SemaphoreType.DMA
    anywhere = pl.BlockSpec(memory_space=pl.ANY)
    smem = pl.BlockSpec(memory_space=pltpu.SMEM)
    out = jax.ShapeDtypeStruct(grad_out.shape, jnp.bfloat16)
    flops = 10 * 2 * heads * length * length * HEAD_DIM
    return pl.pallas_call(
        kernel,
        out_shape=(out, out, out),
        in_specs=[smem, smem] + [anywhere] * 5 + [pl.BlockSpec(memory_space=pltpu.VMEM)],
        out_specs=(anywhere, anywhere, anywhere),
        scratch_shapes=[
            half, half, half, half, half, half, half,
            pltpu.VMEM((heads, length), jnp.float32), row, row,
            wide, wide, wide,
            pltpu.VMEM((3,) + per_head, jnp.bfloat16), half, half,
            dma((4, heads)), dma((heads,)), dma, dma((heads,)), dma((2, 1)), dma((2, heads)),
            dma((2, heads)), dma((2, heads)), dma((2, heads)),
            dma((3,)), dma((3,)), dma((3,)),
        ],
        compiler_params=pltpu.CompilerParams(
            collective_id=0, has_side_effects=True, vmem_limit_bytes=48 * 1024 * 1024
        ),
        cost_estimate=pl.CostEstimate(
            flops=flops, bytes_accessed=8 * length * features * 2, transcendentals=2 * heads * length * length
        ),
        name="attention_backward",
    )(group_length, cache_source, query, key, value, output, grad_out, log_sum)


def solution(mesh):
    by_head, by_token = P("group", None, "head"), P("group", "head", None)
    return jax.shard_map(
        on_device,
        mesh=mesh,
        in_specs=(by_head, by_head, by_head, by_head, by_token, by_token, P(), P()),
        out_specs=(by_token, by_token, by_token),
        check_vma=False,
    )
```

profile of v0, /device:TPU:32, one launch (start us, length us, event | category | flops | bytes accessed | tf_op | source)
XLA Modules:
  0.0 83.4 jit_solution(4454081008317064938)
XLA Ops:
  0.6 0.0 copy-start.6
  0.6 0.0 copy-start.5
  0.7 0.7 copy.11.lse_ref
  1.4 0.0 copy-done.6
  1.4 0.0 copy-done.5
  1.4 0.0 copy-start
  1.4 1.1 %copy-done = bf16[1,512,640]{2,1,0:T(8,128)(2,1)S(1)} copy-done((bf16[1,512,640]{2,1,0:T(8,128)(2,1)S(1)}, bf16[1,512,640]{2,1,0:T(8,128)(2,1)}, u32[]{:S(2)}) %copy-start) | copy-done | bytes 655384
  2.5 0.0 copy-start.1
  2.5 1.1 %copy-done.1 = bf16[1,512,640]{2,1,0:T(8,128)(2,1)S(1)} copy-done((bf16[1,512,640]{2,1,0:T(8,128)(2,1)S(1)}, bf16[1,512,640]{2,1,0:T(8,128)(2,1)}, u32[]{:S(2)}) %copy-start.1) | copy-done | bytes 655384
  3.5 0.0 copy-start.2
  3.6 1.1 %copy-done.2 = bf16[1,512,640]{2,1,0:T(8,128)(2,1)S(1)} copy-done((bf16[1,512,640]{2,1,0:T(8,128)(2,1)S(1)}, bf16[1,512,640]{2,1,0:T(8,128)(2,1)}, u32[]{:S(2)}) %copy-start.2) | copy-done | bytes 655384
  4.6 0.0 copy-start.3
  4.6 1.1 %copy-done.3 = bf16[1,512,640]{2,1,0:T(8,128)(2,1)S(1)} copy-done((bf16[1,512,640]{2,1,0:T(8,128)(2,1)S(1)}, bf16[1,512,640]{2,1,0:T(8,128)(2,1)}, u32[]{:S(2)}) %copy-start.3) | copy-done | bytes 655384
  5.7 0.0 copy-start.4
  5.7 1.1 %copy-done.4 = bf16[1,64,5120]{2,1,0:T(8,128)(2,1)S(1)} copy-done((bf16[1,64,5120]{2,1,0:T(8,128)(2,1)S(1)}, bf16[1,64,5120]{2,1,0:T(8,128)(2,1)}, u32[]{:S(2)}) %copy-start.4) | copy-done | bytes 655384
  6.8 74.1 %attention_backward.1 = (bf16[1,64,5120]{2,1,0:T(8,128)(2,1)S(1)}, bf16[1,64,5120]{2,1,0:T(8,128)(2,1)S(1)}, bf16[1,64,5120]{2,1,0:T(8,128)(2,1)S(1)}) custom-call(s32[32]{0:T(128)S(1)} %copy-done.5, s32[32]{0:T(128)S(1)} %copy-done.6, bf16[1,512,640]{2,1,0:T(8,128)(2,1)S(1)} %copy-done, bf16[1,512,640]{2,1,0:T(8,128)(2,1)S(1)} %copy-done.1, ...), custom_call_target="tpu_custom_call" | custom-call | flops 3355443200 | bytes 5242880 | tf_op jit(solution)/shard_map/attention_backward/pallas_call | solution.py:229
  80.9 0.8 %copy.15 = bf16[1,64,5120]{2,1,0:T(8,128)(2,1)} copy(bf16[1,64,5120]{2,1,0:T(8,128)(2,1)S(1)} %get-tuple-element.6) | data formatting | bytes 1310720
  81.8 0.8 %copy.16 = bf16[1,64,5120]{2,1,0:T(8,128)(2,1)} copy(bf16[1,64,5120]{2,1,0:T(8,128)(2,1)S(1)} %get-tuple-element.7) | data formatting | bytes 1310720
  82.6 0.8 %copy.17 = bf16[1,64,5120]{2,1,0:T(8,128)(2,1)} copy(bf16[1,64,5120]{2,1,0:T(8,128)(2,1)S(1)} %get-tuple-element.8) | data formatting | bytes 1310720
Async XLA Ops:
  0.6 0.7 copy-start.6
  0.6 0.7 copy-start.5
  1.4 1.1 %copy-start = (bf16[1,512,640]{2,1,0:T(8,128)(2,1)S(1)}, bf16[1,512,640]{2,1,0:T(8,128)(2,1)}, u32[]{:S(2)}) copy-start(bf16[1,512,640]{2,1,0:T(8,128)(2,1)} %q_hbm.1) | copy-start | bytes 1966084
  2.5 1.1 %copy-start.1 = (bf16[1,512,640]{2,1,0:T(8,128)(2,1)S(1)}, bf16[1,512,640]{2,1,0:T(8,128)(2,1)}, u32[]{:S(2)}) copy-start(bf16[1,512,640]{2,1,0:T(8,128)(2,1)} %k_hbm.1) | copy-start | bytes 1966084
  3.5 1.1 %copy-start.2 = (bf16[1,512,640]{2,1,0:T(8,128)(2,1)S(1)}, bf16[1,512,640]{2,1,0:T(8,128)(2,1)}, u32[]{:S(2)}) copy-start(bf16[1,512,640]{2,1,0:T(8,128)(2,1)} %v_hbm.1) | copy-start | bytes 1966084
  4.6 1.1 %copy-start.3 = (bf16[1,512,640]{2,1,0:T(8,128)(2,1)S(1)}, bf16[1,512,640]{2,1,0:T(8,128)(2,1)}, u32[]{:S(2)}) copy-start(bf16[1,512,640]{2,1,0:T(8,128)(2,1)} %o_hbm.1) | copy-start | bytes 1966084
  5.7 1.1 %copy-start.4 = (bf16[1,64,5120]{2,1,0:T(8,128)(2,1)S(1)}, bf16[1,64,5120]{2,1,0:T(8,128)(2,1)}, u32[]{:S(2)}) copy-start(bf16[1,64,5120]{2,1,0:T(8,128)(2,1)} %g_hbm.1) | copy-start | bytes 1966084
where the time goes:
time: 83.8 us; the launch traced here: 83.4 us
  Pallas kernels  74.1 us (88%)
  local copies, waits for them, and re-layouts  8.67 us (10%)
    pallas_call x1, Pallas kernels, on_device(): pl.pallas_call(kernel, out_shape=(out, out, out), in_specs=[smem, smem] +...  74.1 us
    unnamed x18, local copies, waits for them, and re-layouts  8.67 us

commit v1 on v0

v1 whole, which is shorter than its diff:
```python
import functools
import math

import jax
import jax.numpy as jnp
from jax import lax
from jax.experimental import pallas as pl
from jax.experimental.pallas import tpu as pltpu
from jax.sharding import PartitionSpec as P

HEAD_DIM = 128
MESH = pl.DeviceIdType.MESH
SCALE = HEAD_DIM**-0.5
LOG2E = math.log2(math.e)
DEAD = 1e30


def dot_nt(a, b):
    return lax.dot_general(a, b, (((1,), (1,)), ((), ())), preferred_element_type=jnp.float32)


def dot_nn(a, b):
    return jnp.dot(a, b, preferred_element_type=jnp.float32)


def block_grads(q, g, lse_row, delta_row, k, kt, v):
    prob = jnp.exp2(dot_nt(k, q) * (SCALE * LOG2E) - lse_row)
    grad_score = (prob * (dot_nt(v, g) - delta_row)).astype(jnp.bfloat16)
    grad_v = dot_nn(prob.astype(jnp.bfloat16), g)
    grad_k = dot_nn(grad_score, q)
    grad_q = dot_nn(kt, grad_score).T
    return grad_q, grad_k, grad_v


def kernel(
    len_ref, source_ref, q_hbm, k_hbm, v_hbm, o_hbm, g_hbm, lse_ref,
    out_q, out_k, out_v,
    q_own, k_own, v_own, o_own, g_own, moved_a, moved_b, lse_next, delta_own, delta_next,
    acc_q, acc_k, acc_v, stage, cross_out, cross_in, land, land_far,
    load_sem, local_sem, g_send, g_recv, lse_sem, a_sem, b_sem, low_sem, direct_send, delta_sem,
    near_sem, far_send, far_recv, out_send, out_recv, out_local,
):
    heads, length, _ = q_own.shape
    groups = lax.axis_size("group")
    parts = lax.axis_size("head")
    half = parts // 2
    rows = length // parts
    group, me = lax.axis_index("group"), lax.axis_index("head")
    after, before = lax.rem(group + 1, groups), lax.rem(group + groups - 1, groups)
    even = lax.rem(group, 2) == 0
    odd = lax.rem(group, 2) == 1
    lower = me < half
    upper = me >= half
    near = lax.rem(group, 2) * before + (1 - lax.rem(group, 2)) * after
    far = lax.rem(group, 2) * after + (1 - lax.rem(group, 2)) * before

    def lanes(i):
        return pl.ds(pl.multiple_of(i * HEAD_DIM, HEAD_DIM), HEAD_DIM)

    def token_rows(part):
        return pl.ds(pl.multiple_of(part * rows, rows), rows)

    low_rows, high_rows = pl.ds(0, length // 2), pl.ds(length // 2, length // 2)

    def to(src, dst, send, recv, device):
        return pltpu.make_async_remote_copy(
            src_ref=src, dst_ref=dst, send_sem=send, recv_sem=recv,
            device_id=device, device_id_type=MESH,
        )

    def wait_bytes(ref, sem):
        pltpu.make_async_copy(ref, ref, sem).wait()

    def loads(i):
        pairs = ((k_hbm, k_own), (v_hbm, v_own), (q_hbm, q_own), (o_hbm, o_own))
        return [
            pltpu.make_async_copy(src.at[0, :, lanes(i)], dst.at[i], load_sem.at[at, i])
            for at, (src, dst) in enumerate(pairs)
        ]

    def local_g(i):
        return pltpu.make_async_copy(
            g_hbm.at[0, :, lanes(me * heads + i)], g_own.at[i, token_rows(me)], local_sem.at[i]
        )

    def key_copy(i):
        return to(k_hbm.at[0, :, lanes(i)], moved_a.at[i], a_sem.at[0, i], a_sem.at[1, i], (after, me))

    def value_copy(i):
        return to(v_hbm.at[0, :, lanes(i)], moved_b.at[i], b_sem.at[0, i], b_sem.at[1, i], (after, me))

    def query_copy(i):
        return to(q_hbm.at[0, :, lanes(i)], moved_a.at[i], a_sem.at[0, i], a_sem.at[1, i], (before, me))

    def g_high_copy(i):
        return to(
            g_own.at[i, high_rows], moved_b.at[i, high_rows], b_sem.at[0, i], b_sem.at[1, i], (before, me)
        )

    def g_low_copy(i):
        return to(
            g_own.at[i, low_rows], moved_b.at[i, low_rows], low_sem.at[0, i], low_sem.at[1, i], (before, me)
        )

    def delta_copy(i):
        return to(delta_own.at[i], delta_next.at[i], delta_sem.at[0, i], delta_sem.at[1, i], (before, me))

    def near_copy(which, i):
        return to(
            cross_out.at[which, i], cross_in.at[which, i],
            near_sem.at[0, which, i], near_sem.at[1, which, i], (near, me),
        )

    lse_copy = to(lse_ref.at[0], lse_next, lse_sem.at[0], lse_sem.at[1], (before, me))

    barrier = pltpu.get_barrier_semaphore()

    @pl.loop(1, parts)
    def _(step):
        pl.semaphore_signal(
            barrier, inc=1, device_id=(group, lax.rem(me + step, parts)), device_id_type=MESH
        )

    @pl.loop(0, parts)
    def _(part):
        pl.semaphore_signal(barrier, inc=1, device_id=(far, part), device_id_type=MESH)

    pl.semaphore_signal(barrier, inc=1, device_id=(near, me), device_id_type=MESH)

    @pl.loop(0, heads)
    def _(i):
        local_g(i).start()
        for copy in loads(i):
            copy.start()

    pl.semaphore_wait(barrier, 2 * parts)

    @pl.loop(0, heads)
    def _(i):
        @pl.loop(1, parts)
        def _(step):
            peer = lax.rem(me + step, parts)
            to(
                g_hbm.at[0, :, lanes(peer * heads + i)], g_own.at[i, token_rows(me)],
                g_send, g_recv.at[i], (group, peer),
            ).start()

        @pl.when(even & lower)
        def _():
            @pl.loop(0, half)
            def _(step):
                peer = half + lax.rem(me + step, half)
                to(
                    g_hbm.at[0, :, lanes(peer * heads + i)], moved_b.at[i, token_rows(me)],
                    direct_send, low_sem.at[1, i], (before, peer),
                ).start()

        @pl.when(lower)
        def _():
            key_copy(i).start()
            value_copy(i).start()

        @pl.when(upper)
        def _():
            query_copy(i).start()

    own_len, before_len = len_ref[group], len_ref[before]
    linked_len = jnp.where(source_ref[group] == before, own_len, 0)
    after_len = jnp.where(source_ref[after] == group, len_ref[after], 0)
    query_at = lax.broadcasted_iota(jnp.int32, (1, length), 1)
    key_at = lax.broadcasted_iota(jnp.int32, (length, HEAD_DIM), 0)
    zero = jnp.zeros((), jnp.bfloat16)

    def own_row(i, live):
        return jnp.where(query_at < live, lse_ref[0, pl.ds(i, 1), :] * LOG2E, DEAD)

    def live_keys(k, live):
        return jnp.where(key_at < live, k, zero)

    def half_rows(x, live):
        return jnp.where(key_at < live, x, 0.0).astype(jnp.bfloat16)

    def send_out(which, i):
        columns = lanes(me * heads + i)

        @pl.loop(1, parts)
        def _(step):
            peer = lax.rem(me + step, parts)
            to(
                stage.at[which, i, token_rows(peer)], land.at[which, :, columns],
                out_send.at[which], out_recv.at[which], (group, peer),
            ).start()

        pltpu.make_async_copy(
            stage.at[which, i, token_rows(me)], land.at[which, :, columns], out_local.at[which]
        ).start()

    def send_far(which, i):
        columns = lanes(lax.rem(me, half) * heads + i)

        @pl.loop(0, parts)
        def _(step):
            peer = lax.rem(me + step, parts)
            to(
                cross_out.at[which, i, token_rows(peer)], land_far.at[which, :, columns],
                far_send.at[which], far_recv.at[which], (far, peer),
            ).start()

    def wait_g(i):
        wait_bytes(g_own.at[i, pl.ds(0, (parts - 1) * rows)], g_recv.at[i])
        local_g(i).wait()

    def own_delta(i):
        product = g_own[i].astype(jnp.float32) * o_own[i].astype(jnp.float32)
        delta = jnp.sum(product.T, axis=0, keepdims=True)
        delta_own[i] = delta
        return delta

    def own_block(i, delta):
        k = live_keys(k_own[i], own_len)
        return block_grads(q_own[i], g_own[i], own_row(i, own_len), delta, k, k.T, v_own[i])

    @pl.when(lower)
    def _():
        def finish_keys(i):
            near_copy(0, i).wait_recv()
            stage[1, i] = (acc_k[i] + cross_in[0, i].astype(jnp.float32)).astype(jnp.bfloat16)
            send_out(1, i)
            near_copy(1, i).wait_recv()
            stage[2, i] = (acc_v[i] + cross_in[1, i].astype(jnp.float32)).astype(jnp.bfloat16)
            send_out(2, i)

        @pl.loop(0, heads)
        def _(i):
            wait_g(i)
            for copy in loads(i):
                copy.wait()
            grad_q, grad_k, grad_v = own_block(i, own_delta(i))
            acc_q[i] = grad_q
            grad_k = jnp.where(key_at < own_len, grad_k * SCALE, 0.0)
            grad_v = jnp.where(key_at < own_len, grad_v, 0.0)

            @pl.when(even)
            def _():
                acc_k[i] = grad_k
                acc_v[i] = grad_v

            @pl.when(odd)
            def _():
                stage[1, i] = grad_k.astype(jnp.bfloat16)
                send_out(1, i)
                stage[2, i] = grad_v.astype(jnp.bfloat16)
                send_out(2, i)

        @pl.loop(0, heads)
        def _(i):
            key_copy(i).wait_recv()
            value_copy(i).wait_recv()
            k = live_keys(moved_a[i], before_len)
            grad_q, grad_k, grad_v = block_grads(
                q_own[i], g_own[i], own_row(i, linked_len), delta_own[i], k, k.T, moved_b[i]
            )
            cross_out[0, i] = half_rows(grad_k * SCALE, before_len)
            cross_out[1, i] = half_rows(grad_v, before_len)

            @pl.when(odd)
            def _():
                near_copy(0, i).start()
                near_copy(1, i).start()

            @pl.when(even)
            def _():
                send_far(0, i)
                send_far(1, i)

            stage[0, i] = ((acc_q[i] + grad_q) * SCALE).astype(jnp.bfloat16)
            send_out(0, i)

            @pl.when(even & (i > 0))
            def _():
                finish_keys(i - 1)

        @pl.when(even)
        def _():
            finish_keys(heads - 1)
            wait_bytes(cross_out.at[0], far_send.at[0])
            wait_bytes(cross_out.at[1], far_send.at[1])
            wait_bytes(g_hbm.at[0, :, pl.ds(0, half * heads * HEAD_DIM)], direct_send)

        @pl.loop(0, heads)
        def _(i):
            key_copy(i).wait_send()
            value_copy(i).wait_send()

            @pl.when(odd)
            def _():
                near_copy(0, i).wait_send()
                near_copy(1, i).wait_send()

    @pl.when(upper)
    def _():
        lse_copy.start()

        def finish_query(i):
            near_copy(0, i).wait_recv()
            stage[0, i] = (acc_q[i] * SCALE + cross_in[0, i].astype(jnp.float32)).astype(jnp.bfloat16)
            send_out(0, i)

        @pl.loop(0, heads)
        def _(i):
            wait_g(i)
            g_high_copy(i).start()

            @pl.when(odd)
            def _():
                g_low_copy(i).start()

            for copy in loads(i):
                copy.wait()
            delta = own_delta(i)
            delta_copy(i).start()
            grad_q, grad_k, grad_v = own_block(i, delta)
            acc_k[i] = grad_k
            acc_v[i] = grad_v

            @pl.when(even)
            def _():
                stage[0, i] = (grad_q * SCALE).astype(jnp.bfloat16)
                send_out(0, i)

            @pl.when(odd)
            def _():
                acc_q[i] = grad_q

        lse_copy.wait_recv()

        @pl.loop(0, heads)
        def _(i):
            query_copy(i).wait_recv()
            g_high_copy(i).wait_recv()
            g_low_copy(i).wait_recv()
            delta_copy(i).wait_recv()
            lse_row = jnp.where(query_at < after_len, lse_next[pl.ds(i, 1), :] * LOG2E, DEAD)
            k = live_keys(k_own[i], own_len)
            grad_q, grad_k, grad_v = block_grads(
                moved_a[i], moved_b[i], lse_row, delta_next[i], k, k.T, v_own[i]
            )
            cross_out[0, i] = (grad_q * SCALE).astype(jnp.bfloat16)

            @pl.when(even)
            def _():
                near_copy(0, i).start()

            @pl.when(odd)
            def _():
                send_far(0, i)

            stage[1, i] = half_rows((acc_k[i] + grad_k) * SCALE, own_len)
            send_out(1, i)
            stage[2, i] = half_rows(acc_v[i] + grad_v, own_len)
            send_out(2, i)

            @pl.when(odd & (i > 0))
            def _():
                finish_query(i - 1)

        @pl.when(odd)
        def _():
            finish_query(heads - 1)
            wait_bytes(cross_out.at[0], far_send.at[0])

        lse_copy.wait_send()

        @pl.loop(0, heads)
        def _(i):
            query_copy(i).wait_send()
            g_high_copy(i).wait_send()
            delta_copy(i).wait_send()

            @pl.when(odd)
            def _():
                g_low_copy(i).wait_send()

            @pl.when(even)
            def _():
                near_copy(0, i).wait_send()

    wait_bytes(g_hbm.at[0, :, pl.ds(0, (parts - 1) * heads * HEAD_DIM)], g_send)
    for which in range(3):
        theirs = land.at[which, :, pl.ds(0, (parts - 1) * heads * HEAD_DIM)]
        wait_bytes(theirs, out_recv.at[which])
        wait_bytes(theirs, out_send.at[which])
        wait_bytes(land.at[which, :, pl.ds(0, heads * HEAD_DIM)], out_local.at[which])

    low = pl.ds(0, half * heads * HEAD_DIM)
    high = pl.ds(half * heads * HEAD_DIM, half * heads * HEAD_DIM)

    def summed(which, columns, far_at):
        total = land[which, :, columns].astype(jnp.float32) + land_far[far_at].astype(jnp.float32)
        return total.astype(jnp.bfloat16)

    wait_bytes(land_far.at[0], far_recv.at[0])
    out_q[0, :, low] = land[0, :, low]
    out_k[0, :, high] = land[1, :, high]
    out_v[0, :, high] = land[2, :, high]

    @pl.when(even)
    def _():
        out_q[0, :, high] = summed(0, high, 0)
        out_k[0, :, low] = land[1, :, low]
        out_v[0, :, low] = land[2, :, low]

    @pl.when(odd)
    def _():
        wait_bytes(land_far.at[1], far_recv.at[1])
        out_q[0, :, high] = land[0, :, high]
        out_k[0, :, low] = summed(1, low, 0)
        out_v[0, :, low] = summed(2, low, 1)


def on_device(query, key, value, output, grad_out, log_sum, group_length, cache_source):
    _, length, features = query.shape
    heads = features // HEAD_DIM
    per_head = (heads, length, HEAD_DIM)
    half = pltpu.VMEM(per_head, jnp.bfloat16)
    wide = pltpu.VMEM(per_head, jnp.float32)
    row = pltpu.VMEM((heads, 1, length), jnp.float32)
    dma = pltpu.SemaphoreType.DMA
    anywhere = pl.BlockSpec(memory_space=pl.ANY)
    smem = pl.BlockSpec(memory_space=pltpu.SMEM)
    vmem = pl.BlockSpec(memory_space=pltpu.VMEM)
    out = jax.ShapeDtypeStruct(grad_out.shape, jnp.bfloat16)
    flops = 10 * 2 * heads * length * length * HEAD_DIM
    return pl.pallas_call(
        kernel,
        out_shape=(out, out, out),
        in_specs=[smem, smem] + [anywhere] * 5 + [vmem],
        out_specs=(vmem, vmem, vmem),
        scratch_shapes=[
            half, half, half, half, half, half, half,
            pltpu.VMEM((heads, length), jnp.float32), row, row,
            wide, wide, wide,
            pltpu.VMEM((3,) + per_head, jnp.bfloat16), pltpu.VMEM((2,) + per_head, jnp.bfloat16),
            pltpu.VMEM((2,) + per_head, jnp.bfloat16),
            pltpu.VMEM((3,) + grad_out.shape[1:], jnp.bfloat16),
            pltpu.VMEM((2, grad_out.shape[1], grad_out.shape[2] // 2), jnp.bfloat16),
            dma((4, heads)), dma((heads,)), dma, dma((heads,)), dma((2,)), dma((2, heads)),
            dma((2, heads)), dma((2, heads)), dma, dma((2, heads)),
            dma((2, 2, heads)), dma((2,)), dma((2,)), dma((3,)), dma((3,)), dma((3,)),
        ],
        compiler_params=pltpu.CompilerParams(
            collective_id=0, has_side_effects=True, vmem_limit_bytes=60 * 1024 * 1024
        ),
        cost_estimate=pl.CostEstimate(
            flops=flops, bytes_accessed=8 * length * features * 2, transcendentals=2 * heads * length * length
        ),
        name="attention_backward",
    )(group_length, cache_source, query, key, value, output, grad_out, log_sum)


def solution(mesh):
    by_head, by_token = P("group", None, "head"), P("group", "head", None)
    return jax.shard_map(
        on_device,
        mesh=mesh,
        in_specs=(by_head, by_head, by_head, by_head, by_token, by_token, P(), P()),
        out_specs=(by_token, by_token, by_token),
        check_vma=False,
    )
```

time: 83.8 us -> 67.1 us (0.80)
  the two profiles are of different devices: /device:TPU:32 before, /device:TPU:1 now
where the time goes in v1:
time: 67.1 us; the launch traced here: 66.8 us
  Pallas kernels  60.7 us (90%)
  local copies, waits for them, and re-layouts  5.5 us (8%)
    pallas_call x1, Pallas kernels, on_device(): pl.pallas_call(kernel, out_shape=(out, out, out), in_specs=[smem, smem] +...  60.7 us
    unnamed x8, local copies, waits for them, and re-layouts  5.5 us

profile of v1, /device:TPU:1, one launch (start us, length us, event | category | flops | bytes accessed | tf_op | source)
XLA Modules:
  0.0 66.8 jit_solution(17247586031692060627)
XLA Ops:
  0.6 1.3 %copy.11.lse_ref = f32[1,5,512]{2,1,0:T(8,128)} copy(f32[1,5,512]{2,0,1:T(1,128)} %param.13) | data formatting | bytes 20480 | tf_op args[5]
  1.9 60.7 %attention_backward.1 = (bf16[1,64,5120]{2,1,0:T(8,128)(2,1)}, bf16[1,64,5120]{2,1,0:T(8,128)(2,1)}, bf16[1,64,5120]{2,1,0:T(8,128)(2,1)}) custom-call(s32[32]{0:T(128)} %len_ref.1, s32[32]{0:T(128)} %source_ref.1, bf16[1,512,640]{2,1,0:T(8,128)(2,1)} %q_hbm.1, bf16[1,512,640]{2,1,0:T(8,128)(2,1)} %k_hbm.1, bf16[1,512,640]{2,1,0:T(8,128)(2,1)} %v_hbm.1, ...), custom_call_target="tpu_custom_call" | custom-call | flops 3355443200 | bytes 5242880 | tf_op jit(solution)/shard_map/attention_backward/pallas_call | solution.py:434
  62.6 0.0 copy-start.1
  62.6 2.0 %copy.15 = bf16[1,64,5120]{2,1,0:T(8,128)(2,1)} copy(bf16[1,64,5120]{2,1,0:T(8,128)(2,1)} %get-tuple-element.6) | data formatting | bytes 1310720
  64.7 0.0 copy-done.1
  64.7 0.0 copy-start
  64.7 0.8 %copy.16 = bf16[1,64,5120]{2,1,0:T(8,128)(2,1)} copy(bf16[1,64,5120]{2,1,0:T(8,128)(2,1)S(1)} %copy-done.1) | data formatting | bytes 1310720
  65.5 0.5 copy-done
  66.0 0.8 %copy.17 = bf16[1,64,5120]{2,1,0:T(8,128)(2,1)} copy(bf16[1,64,5120]{2,1,0:T(8,128)(2,1)S(1)} %copy-done) | data formatting | bytes 1310720
Async XLA Ops:
  62.6 2.0 %copy-start.1 = (bf16[1,64,5120]{2,1,0:T(8,128)(2,1)S(1)}, bf16[1,64,5120]{2,1,0:T(8,128)(2,1)}, u32[]{:S(2)}) copy-start(bf16[1,64,5120]{2,1,0:T(8,128)(2,1)} %get-tuple-element.7) | copy-start | bytes 1966084
  64.7 1.3 %copy-start = (bf16[1,64,5120]{2,1,0:T(8,128)(2,1)S(1)}, bf16[1,64,5120]{2,1,0:T(8,128)(2,1)}, u32[]{:S(2)}) copy-start(bf16[1,64,5120]{2,1,0:T(8,128)(2,1)} %get-tuple-element.8) | copy-start | bytes 1966084

commit v2 on v1

--- a/solution.py
+++ b/solution.py
@@ -33,11 +33,11 @@
 
 
 def kernel(
-    len_ref, source_ref, q_hbm, k_hbm, v_hbm, o_hbm, g_hbm, lse_ref,
+    len_hbm, source_hbm, q_hbm, k_hbm, v_hbm, o_hbm, g_hbm, lse_hbm,
     out_q, out_k, out_v,
-    q_own, k_own, v_own, o_own, g_own, moved_a, moved_b, lse_next, delta_own, delta_next,
+    len_ref, source_ref, q_own, k_own, v_own, o_own, g_own, moved_a, moved_b, lse_own, lse_next, delta_own, delta_next,
     acc_q, acc_k, acc_v, stage, cross_out, cross_in, land, land_far,
-    load_sem, local_sem, g_send, g_recv, lse_sem, a_sem, b_sem, low_sem, direct_send, delta_sem,
+    load_sem, local_sem, g_send, g_recv, small_load, lse_sem, a_sem, b_sem, low_sem, direct_send, delta_sem,
     near_sem, far_send, far_recv, out_send, out_recv, out_local,
 ):
     heads, length, _ = q_own.shape
@@ -111,8 +111,12 @@
             near_sem.at[0, which, i], near_sem.at[1, which, i], (near, me),
         )
 
-    lse_copy = to(lse_ref.at[0], lse_next, lse_sem.at[0], lse_sem.at[1], (before, me))
-
+    lse_copy = to(lse_hbm, lse_next, lse_sem.at[0], lse_sem.at[1], (before, me))
+
+    small = ((lse_hbm, lse_own), (len_hbm, len_ref), (source_hbm, source_ref))
+    small_loads = [pltpu.make_async_copy(src, dst, small_load.at[i]) for i, (src, dst) in enumerate(small)]
+    for copy in small_loads:
+        copy.start()
     barrier = pltpu.get_barrier_semaphore()
 
     @pl.loop(1, parts)
@@ -164,6 +168,8 @@
         def _():
             query_copy(i).start()
 
+    for copy in small_loads:
+        copy.wait()
     own_len, before_len = len_ref[group], len_ref[before]
     linked_len = jnp.where(source_ref[group] == before, own_len, 0)
     after_len = jnp.where(source_ref[after] == group, len_ref[after], 0)
@@ -172,7 +178,7 @@
     zero = jnp.zeros((), jnp.bfloat16)
 
     def own_row(i, live):
-        return jnp.where(query_at < live, lse_ref[0, pl.ds(i, 1), :] * LOG2E, DEAD)
+        return jnp.where(query_at < live, lse_own[i] * LOG2E, DEAD)
 
     def live_keys(k, live):
         return jnp.where(key_at < live, k, zero)
@@ -340,7 +346,7 @@
             g_high_copy(i).wait_recv()
             g_low_copy(i).wait_recv()
             delta_copy(i).wait_recv()
-            lse_row = jnp.where(query_at < after_len, lse_next[pl.ds(i, 1), :] * LOG2E, DEAD)
+            lse_row = jnp.where(query_at < after_len, lse_next[i] * LOG2E, DEAD)
             k = live_keys(k_own[i], own_len)
             grad_q, grad_k, grad_v = block_grads(
                 moved_a[i], moved_b[i], lse_row, delta_next[i], k, k.T, v_own[i]
@@ -416,6 +422,15 @@
         out_q[0, :, high] = land[0, :, high]
         out_k[0, :, low] = summed(1, low, 0)
         out_v[0, :, low] = summed(2, low, 1)
+
+
+def write_kernel(in_q, in_k, in_v, out_q, out_k, out_v, sems):
+    pairs = ((in_q, out_q), (in_k, out_k), (in_v, out_v))
+    copies = [pltpu.make_async_copy(src, dst, sems.at[i]) for i, (src, dst) in enumerate(pairs)]
+    for copy in copies:
+        copy.start()
+    for copy in copies:
+        copy.wait()
 
 
 def on_device(query, key, value, output, grad_out, log_sum, group_length, cache_source):
@@ -427,35 +442,47 @@
     row = pltpu.VMEM((heads, 1, length), jnp.float32)
     dma = pltpu.SemaphoreType.DMA
     anywhere = pl.BlockSpec(memory_space=pl.ANY)
-    smem = pl.BlockSpec(memory_space=pltpu.SMEM)
     vmem = pl.BlockSpec(memory_space=pltpu.VMEM)
     out = jax.ShapeDtypeStruct(grad_out.shape, jnp.bfloat16)
     flops = 10 * 2 * heads * length * length * HEAD_DIM
-    return pl.pallas_call(
+    rows_first = log_sum.transpose(1, 0, 2)
+    inputs = (group_length, cache_source, query, key, value, output, grad_out, rows_first)
+    landed = pl.pallas_call(
         kernel,
         out_shape=(out, out, out),
-        in_specs=[smem, smem] + [anywhere] * 5 + [vmem],
+        in_specs=[anywhere] * 8,
         out_specs=(vmem, vmem, vmem),
         scratch_shapes=[
+            pltpu.SMEM(group_length.shape, jnp.int32), pltpu.SMEM(cache_source.shape, jnp.int32),
             half, half, half, half, half, half, half,
-            pltpu.VMEM((heads, length), jnp.float32), row, row,
+            row, row, row, row,
             wide, wide, wide,
             pltpu.VMEM((3,) + per_head, jnp.bfloat16), pltpu.VMEM((2,) + per_head, jnp.bfloat16),
             pltpu.VMEM((2,) + per_head, jnp.bfloat16),
             pltpu.VMEM((3,) + grad_out.shape[1:], jnp.bfloat16),
             pltpu.VMEM((2, grad_out.shape[1], grad_out.shape[2] // 2), jnp.bfloat16),
-            dma((4, heads)), dma((heads,)), dma, dma((heads,)), dma((2,)), dma((2, heads)),
+            dma((4, heads)), dma((heads,)), dma, dma((heads,)), dma((3,)), dma((2,)), dma((2, heads)),
             dma((2, heads)), dma((2, heads)), dma, dma((2, heads)),
             dma((2, 2, heads)), dma((2,)), dma((2,)), dma((3,)), dma((3,)), dma((3,)),
         ],
         compiler_params=pltpu.CompilerParams(
-            collective_id=0, has_side_effects=True, vmem_limit_bytes=60 * 1024 * 1024
+            collective_id=0, has_side_effects=True, vmem_limit_bytes=40 * 1024 * 1024
         ),
         cost_estimate=pl.CostEstimate(
             flops=flops, bytes_accessed=8 * length * features * 2, transcendentals=2 * heads * length * length
         ),
         name="attention_backward",
-    )(group_length, cache_source, query, key, value, output, grad_out, log_sum)
+    )(*[pltpu.with_memory_space_constraint(x, pltpu.HBM) for x in inputs])
+    return pl.pallas_call(
+        write_kernel,
+        out_shape=(out, out, out),
+        in_specs=[vmem] * 3,
+        out_specs=(anywhere, anywhere, anywhere),
+        scratch_shapes=[dma((3,))],
+        cost_estimate=pl.CostEstimate(flops=0, bytes_accessed=6 * out.size * 2, transcendentals=0),
+        compiler_params=pltpu.CompilerParams(vmem_limit_bytes=16 * 1024 * 1024),
+        name="write_out",
+    )(*landed)
 
 
 def solution(mesh):

time: 67.1 us -> 60.8 us (0.906)
  local copies, waits for them, and re-layouts: 5.5 us -> 0 us
    unnamed x8 -> x0, local copies, waits for them, and re-layouts: 5.5 us -> none
    pallas_call x1 -> x2, Pallas kernels: 60.7 us -> 60.1 us  [the longest x1 58.8 us: on_device(): pl.pallas_call(kernel, out_shape=(out, out, out), in_specs=[anywhere] * 8...]
where the time goes in v2:
time: 60.8 us; the launch traced here: 60.7 us
  Pallas kernels  60.1 us (99%)
  between operations  0.64 us (1%)
    pallas_call x1, Pallas kernels, on_device(): pl.pallas_call(kernel, out_shape=(out, out, out), in_specs=[anywhere] * 8...  58.8 us
    pallas_call x1, Pallas kernels, on_device(): pl.pallas_call(write_kernel, out_shape=(out, out, out), in_specs=[vmem] *...  1.3 us

profile of v2, /device:TPU:1, one launch (start us, length us, event | category | flops | bytes accessed | tf_op | source)
XLA Modules:
  0.0 60.7 jit_solution(8536413897804601660)
XLA Ops:
  0.6 58.8 %attention_backward.1 = (bf16[1,64,5120]{2,1,0:T(8,128)(2,1)S(1)}, bf16[1,64,5120]{2,1,0:T(8,128)(2,1)S(1)}, bf16[1,64,5120]{2,1,0:T(8,128)(2,1)S(1)}) custom-call(s32[32]{0:T(128)} %len_hbm.1, s32[32]{0:T(128)} %source_hbm.1, bf16[1,512,640]{2,1,0:T(8,128)(2,1)} %q_hbm.1, bf16[1,512,640]{2,1,0:T(8,128)(2,1)} %k_hbm.1, bf16[1,512,640]{2,1,0:T(8,128)(2,1)} %v_hbm.1, ...), custom_call_target="tpu_custom_call" | custom-call | flops 3355443200 | bytes 5242880 | tf_op jit(solution)/shard_map/attention_backward/pallas_call | solution.py:450
  59.4 1.3 %write_out.1 = (bf16[1,64,5120]{2,1,0:T(8,128)(2,1)}, bf16[1,64,5120]{2,1,0:T(8,128)(2,1)}, bf16[1,64,5120]{2,1,0:T(8,128)(2,1)}) custom-call(bf16[1,64,5120]{2,1,0:T(8,128)(2,1)S(1)} %get-tuple-element.6.in_q, bf16[1,64,5120]{2,1,0:T(8,128)(2,1)S(1)} %get-tuple-element.7.in_k, bf16[1,64,5120]{2,1,0:T(8,128)(2,1)S(1)} %get-tuple-element.8.in_v), custom_call_target="tpu_custom_call" | custom-call | bytes 3932160 | tf_op jit(solution)/shard_map/write_out/pallas_call | solution.py:476

commit v3 on v2

--- a/solution.py
+++ b/solution.py
@@ -36,11 +36,12 @@
     len_hbm, source_hbm, q_hbm, k_hbm, v_hbm, o_hbm, g_hbm, lse_hbm,
     out_q, out_k, out_v,
     len_ref, source_ref, q_own, k_own, v_own, o_own, g_own, moved_a, moved_b, lse_own, lse_next, delta_own, delta_next,
-    acc_q, acc_k, acc_v, stage, cross_out, cross_in, land, land_far,
+    acc_q, acc_k, acc_v, stage, cross_out, cross_in, land_far,
     load_sem, local_sem, g_send, g_recv, small_load, lse_sem, a_sem, b_sem, low_sem, direct_send, delta_sem,
-    near_sem, far_send, far_recv, out_send, out_recv, out_local,
+    near_sem, far_send, far_recv, out_send, out_recv, out_local, far_ready,
 ):
     heads, length, _ = q_own.shape
+    outs = (out_q, out_k, out_v)
     groups = lax.axis_size("group")
     parts = lax.axis_size("head")
     half = parts // 2
@@ -51,6 +52,8 @@
     odd = lax.rem(group, 2) == 1
     lower = me < half
     upper = me >= half
+    has_before, has_after = group > 0, group < groups - 1
+    has_far = has_before & has_after
     near = lax.rem(group, 2) * before + (1 - lax.rem(group, 2)) * after
     far = lax.rem(group, 2) * after + (1 - lax.rem(group, 2)) * before
 
@@ -113,10 +116,6 @@
 
     lse_copy = to(lse_hbm, lse_next, lse_sem.at[0], lse_sem.at[1], (before, me))
 
-    small = ((lse_hbm, lse_own), (len_hbm, len_ref), (source_hbm, source_ref))
-    small_loads = [pltpu.make_async_copy(src, dst, small_load.at[i]) for i, (src, dst) in enumerate(small)]
-    for copy in small_loads:
-        copy.start()
     barrier = pltpu.get_barrier_semaphore()
 
     @pl.loop(1, parts)
@@ -125,19 +124,25 @@
             barrier, inc=1, device_id=(group, lax.rem(me + step, parts)), device_id_type=MESH
         )
 
-    @pl.loop(0, parts)
-    def _(part):
-        pl.semaphore_signal(barrier, inc=1, device_id=(far, part), device_id_type=MESH)
-
     pl.semaphore_signal(barrier, inc=1, device_id=(near, me), device_id_type=MESH)
 
-    @pl.loop(0, heads)
-    def _(i):
-        local_g(i).start()
-        for copy in loads(i):
-            copy.start()
-
-    pl.semaphore_wait(barrier, 2 * parts)
+    def greet_far(sem):
+        @pl.loop(0, parts)
+        def _(part):
+            pl.semaphore_signal(sem, inc=1, device_id=(far, part), device_id_type=MESH)
+
+    @pl.when(odd & has_far)
+    def _():
+        pl.semaphore_wait(barrier, 2 * parts)
+        greet_far(far_ready)
+
+    @pl.when(even | jnp.logical_not(has_far))
+    def _():
+        pl.semaphore_wait(barrier, parts)
+
+    @pl.when(even & has_far)
+    def _():
+        greet_far(barrier)
 
     @pl.loop(0, heads)
     def _(i):
@@ -149,7 +154,13 @@
                 g_send, g_recv.at[i], (group, peer),
             ).start()
 
-        @pl.when(even & lower)
+    @pl.when(even & has_far)
+    def _():
+        pl.semaphore_wait(far_ready, parts)
+
+    @pl.loop(0, heads)
+    def _(i):
+        @pl.when(even & lower & has_before)
         def _():
             @pl.loop(0, half)
             def _(step):
@@ -159,14 +170,26 @@
                     direct_send, low_sem.at[1, i], (before, peer),
                 ).start()
 
-        @pl.when(lower)
+    @pl.loop(0, heads)
+    def _(i):
+        @pl.when(lower & has_after)
         def _():
             key_copy(i).start()
             value_copy(i).start()
 
-        @pl.when(upper)
+        @pl.when(upper & has_before)
         def _():
             query_copy(i).start()
+
+    small = ((lse_hbm, lse_own), (len_hbm, len_ref), (source_hbm, source_ref))
+    small_loads = [pltpu.make_async_copy(src, dst, small_load.at[i]) for i, (src, dst) in enumerate(small)]
+    for copy in small_loads:
+        copy.start()
+    @pl.loop(0, heads)
+    def _(i):
+        local_g(i).start()
+        for copy in loads(i):
+            copy.start()
 
     for copy in small_loads:
         copy.wait()
@@ -193,12 +216,12 @@
         def _(step):
             peer = lax.rem(me + step, parts)
             to(
-                stage.at[which, i, token_rows(peer)], land.at[which, :, columns],
+                stage.at[which, i, token_rows(peer)], outs[which].at[0, :, columns],
                 out_send.at[which], out_recv.at[which], (group, peer),
             ).start()
 
         pltpu.make_async_copy(
-            stage.at[which, i, token_rows(me)], land.at[which, :, columns], out_local.at[which]
+            stage.at[which, i, token_rows(me)], outs[which].at[0, :, columns], out_local.at[which]
         ).start()
 
     def send_far(which, i):
@@ -260,26 +283,33 @@
 
         @pl.loop(0, heads)
         def _(i):
-            key_copy(i).wait_recv()
-            value_copy(i).wait_recv()
-            k = live_keys(moved_a[i], before_len)
-            grad_q, grad_k, grad_v = block_grads(
-                q_own[i], g_own[i], own_row(i, linked_len), delta_own[i], k, k.T, moved_b[i]
-            )
-            cross_out[0, i] = half_rows(grad_k * SCALE, before_len)
-            cross_out[1, i] = half_rows(grad_v, before_len)
-
-            @pl.when(odd)
-            def _():
-                near_copy(0, i).start()
-                near_copy(1, i).start()
-
-            @pl.when(even)
-            def _():
-                send_far(0, i)
-                send_far(1, i)
-
-            stage[0, i] = ((acc_q[i] + grad_q) * SCALE).astype(jnp.bfloat16)
+            @pl.when(has_before)
+            def _():
+                key_copy(i).wait_recv()
+                value_copy(i).wait_recv()
+                k = live_keys(moved_a[i], before_len)
+                grad_q, grad_k, grad_v = block_grads(
+                    q_own[i], g_own[i], own_row(i, linked_len), delta_own[i], k, k.T, moved_b[i]
+                )
+                cross_out[0, i] = half_rows(grad_k * SCALE, before_len)
+                cross_out[1, i] = half_rows(grad_v, before_len)
+
+                @pl.when(odd)
+                def _():
+                    near_copy(0, i).start()
+                    near_copy(1, i).start()
+
+                @pl.when(even)
+                def _():
+                    send_far(0, i)
+                    send_far(1, i)
+
+                stage[0, i] = ((acc_q[i] + grad_q) * SCALE).astype(jnp.bfloat16)
+
+            @pl.when(jnp.logical_not(has_before))
+            def _():
+                stage[0, i] = (acc_q[i] * SCALE).astype(jnp.bfloat16)
+
             send_out(0, i)
 
             @pl.when(even & (i > 0))
@@ -289,14 +319,19 @@
         @pl.when(even)
         def _():
             finish_keys(heads - 1)
+
+        @pl.when(even & has_before)
+        def _():
             wait_bytes(cross_out.at[0], far_send.at[0])
             wait_bytes(cross_out.at[1], far_send.at[1])
             wait_bytes(g_hbm.at[0, :, pl.ds(0, half * heads * HEAD_DIM)], direct_send)
 
         @pl.loop(0, heads)
         def _(i):
-            key_copy(i).wait_send()
-            value_copy(i).wait_send()
+            @pl.when(has_after)
+            def _():
+                key_copy(i).wait_send()
+                value_copy(i).wait_send()
 
             @pl.when(odd)
             def _():
@@ -305,7 +340,9 @@
 
     @pl.when(upper)
     def _():
-        lse_copy.start()
+        @pl.when(has_before)
+        def _():
+            lse_copy.start()
 
         def finish_query(i):
             near_copy(0, i).wait_recv()
@@ -315,7 +352,9 @@
         @pl.loop(0, heads)
         def _(i):
             wait_g(i)
-            g_high_copy(i).start()
+            @pl.when(has_before)
+            def _():
+                g_high_copy(i).start()
 
             @pl.when(odd)
             def _():
@@ -324,7 +363,11 @@
             for copy in loads(i):
                 copy.wait()
             delta = own_delta(i)
-            delta_copy(i).start()
+
+            @pl.when(has_before)
+            def _():
+                delta_copy(i).start()
+
             grad_q, grad_k, grad_v = own_block(i, delta)
             acc_k[i] = grad_k
             acc_v[i] = grad_v
@@ -338,32 +381,42 @@
             def _():
                 acc_q[i] = grad_q
 
-        lse_copy.wait_recv()
+        @pl.when(has_after)
+        def _():
+            lse_copy.wait_recv()
 
         @pl.loop(0, heads)
         def _(i):
-            query_copy(i).wait_recv()
-            g_high_copy(i).wait_recv()
-            g_low_copy(i).wait_recv()
-            delta_copy(i).wait_recv()
-            lse_row = jnp.where(query_at < after_len, lse_next[i] * LOG2E, DEAD)
-            k = live_keys(k_own[i], own_len)
-            grad_q, grad_k, grad_v = block_grads(
-                moved_a[i], moved_b[i], lse_row, delta_next[i], k, k.T, v_own[i]
-            )
-            cross_out[0, i] = (grad_q * SCALE).astype(jnp.bfloat16)
-
-            @pl.when(even)
-            def _():
-                near_copy(0, i).start()
-
-            @pl.when(odd)
-            def _():
-                send_far(0, i)
-
-            stage[1, i] = half_rows((acc_k[i] + grad_k) * SCALE, own_len)
+            @pl.when(has_after)
+            def _():
+                query_copy(i).wait_recv()
+                g_high_copy(i).wait_recv()
+                g_low_copy(i).wait_recv()
+                delta_copy(i).wait_recv()
+                lse_row = jnp.where(query_at < after_len, lse_next[i] * LOG2E, DEAD)
+                k = live_keys(k_own[i], own_len)
+                grad_q, grad_k, grad_v = block_grads(
+                    moved_a[i], moved_b[i], lse_row, delta_next[i], k, k.T, v_own[i]
+                )
+                cross_out[0, i] = (grad_q * SCALE).astype(jnp.bfloat16)
+
+                @pl.when(even)
+                def _():
+                    near_copy(0, i).start()
+
+                @pl.when(odd)
+                def _():
+                    send_far(0, i)
+
+                stage[1, i] = half_rows((acc_k[i] + grad_k) * SCALE, own_len)
+                stage[2, i] = half_rows(acc_v[i] + grad_v, own_len)
+
+            @pl.when(jnp.logical_not(has_after))
+            def _():
+                stage[1, i] = half_rows(acc_k[i] * SCALE, own_len)
+                stage[2, i] = half_rows(acc_v[i], own_len)
+
             send_out(1, i)
-            stage[2, i] = half_rows(acc_v[i] + grad_v, own_len)
             send_out(2, i)
 
             @pl.when(odd & (i > 0))
@@ -373,15 +426,22 @@
         @pl.when(odd)
         def _():
             finish_query(heads - 1)
+
+        @pl.when(odd & has_after)
+        def _():
             wait_bytes(cross_out.at[0], far_send.at[0])
 
-        lse_copy.wait_send()
+        @pl.when(has_before)
+        def _():
+            lse_copy.wait_send()
 
         @pl.loop(0, heads)
         def _(i):
-            query_copy(i).wait_send()
-            g_high_copy(i).wait_send()
-            delta_copy(i).wait_send()
+            @pl.when(has_before)
+            def _():
+                query_copy(i).wait_send()
+                g_high_copy(i).wait_send()
+                delta_copy(i).wait_send()
 
             @pl.when(odd)
             def _():
@@ -393,35 +453,31 @@
 
     wait_bytes(g_hbm.at[0, :, pl.ds(0, (parts - 1) * heads * HEAD_DIM)], g_send)
     for which in range(3):
-        theirs = land.at[which, :, pl.ds(0, (parts - 1) * heads * HEAD_DIM)]
+        theirs = outs[which].at[0, :, pl.ds(0, (parts - 1) * heads * HEAD_DIM)]
         wait_bytes(theirs, out_recv.at[which])
         wait_bytes(theirs, out_send.at[which])
-        wait_bytes(land.at[which, :, pl.ds(0, heads * HEAD_DIM)], out_local.at[which])
+        wait_bytes(outs[which].at[0, :, pl.ds(0, heads * HEAD_DIM)], out_local.at[which])
 
     low = pl.ds(0, half * heads * HEAD_DIM)
     high = pl.ds(half * heads * HEAD_DIM, half * heads * HEAD_DIM)
 
-    def summed(which, columns, far_at):
-        total = land[which, :, columns].astype(jnp.float32) + land_far[far_at].astype(jnp.float32)
-        return total.astype(jnp.bfloat16)
-
-    wait_bytes(land_far.at[0], far_recv.at[0])
-    out_q[0, :, low] = land[0, :, low]
-    out_k[0, :, high] = land[1, :, high]
-    out_v[0, :, high] = land[2, :, high]
-
-    @pl.when(even)
-    def _():
-        out_q[0, :, high] = summed(0, high, 0)
-        out_k[0, :, low] = land[1, :, low]
-        out_v[0, :, low] = land[2, :, low]
-
-    @pl.when(odd)
+    def add_far(out, columns, far_at):
+        total = out[0, :, columns].astype(jnp.float32) + land_far[far_at].astype(jnp.float32)
+        out[0, :, columns] = total.astype(jnp.bfloat16)
+
+    @pl.when(has_far)
+    def _():
+        wait_bytes(land_far.at[0], far_recv.at[0])
+
+    @pl.when(even & has_far)
+    def _():
+        add_far(out_q, high, 0)
+
+    @pl.when(odd & has_far)
     def _():
         wait_bytes(land_far.at[1], far_recv.at[1])
-        out_q[0, :, high] = land[0, :, high]
-        out_k[0, :, low] = summed(1, low, 0)
-        out_v[0, :, low] = summed(2, low, 1)
+        add_far(out_k, low, 0)
+        add_far(out_v, low, 1)
 
 
 def write_kernel(in_q, in_k, in_v, out_q, out_k, out_v, sems):
@@ -459,11 +515,11 @@
             wide, wide, wide,
             pltpu.VMEM((3,) + per_head, jnp.bfloat16), pltpu.VMEM((2,) + per_head, jnp.bfloat16),
             pltpu.VMEM((2,) + per_head, jnp.bfloat16),
-            pltpu.VMEM((3,) + grad_out.shape[1:], jnp.bfloat16),
             pltpu.VMEM((2, grad_out.shape[1], grad_out.shape[2] // 2), jnp.bfloat16),
             dma((4, heads)), dma((heads,)), dma, dma((heads,)), dma((3,)), dma((2,)), dma((2, heads)),
             dma((2, heads)), dma((2, heads)), dma, dma((2, heads)),
             dma((2, 2, heads)), dma((2,)), dma((2,)), dma((3,)), dma((3,)), dma((3,)),
+            pltpu.SemaphoreType.REGULAR,
         ],
         compiler_params=pltpu.CompilerParams(
             collective_id=0, has_side_effects=True, vmem_limit_bytes=40 * 1024 * 1024

time: 60.8 us -> 58 us (0.954)
  the two profiles are of different devices: /device:TPU:1 before, /device:TPU:7 now
where the time goes in v3:
time: 58 us; the launch traced here: 57.4 us
  Pallas kernels  56.7 us (98%)
  between operations  0.64 us (1%)
    pallas_call x1, Pallas kernels, on_device(): pl.pallas_call(kernel, out_shape=(out, out, out), in_specs=[anywhere] * 8...  55.4 us
    pallas_call x1, Pallas kernels, on_device(): pl.pallas_call(write_kernel, out_shape=(out, out, out), in_specs=[vmem] *...  1.3 us

profile of v3, /device:TPU:7, one launch (start us, length us, event | category | flops | bytes accessed | tf_op | source)
XLA Modules:
  0.0 57.4 jit_solution(16189708609388208905)
XLA Ops:
  0.6 55.4 %attention_backward.1 = (bf16[1,64,5120]{2,1,0:T(8,128)(2,1)S(1)}, bf16[1,64,5120]{2,1,0:T(8,128)(2,1)S(1)}, bf16[1,64,5120]{2,1,0:T(8,128)(2,1)S(1)}) custom-call(s32[32]{0:T(128)} %len_hbm.1, s32[32]{0:T(128)} %source_hbm.1, bf16[1,512,640]{2,1,0:T(8,128)(2,1)} %q_hbm.1, bf16[1,512,640]{2,1,0:T(8,128)(2,1)} %k_hbm.1, bf16[1,512,640]{2,1,0:T(8,128)(2,1)} %v_hbm.1, ...), custom_call_target="tpu_custom_call" | custom-call | flops 3355443200 | bytes 5242880 | tf_op jit(solution)/shard_map/attention_backward/pallas_call | solution.py:506
  56.1 1.3 %write_out.1 = (bf16[1,64,5120]{2,1,0:T(8,128)(2,1)}, bf16[1,64,5120]{2,1,0:T(8,128)(2,1)}, bf16[1,64,5120]{2,1,0:T(8,128)(2,1)}) custom-call(bf16[1,64,5120]{2,1,0:T(8,128)(2,1)S(1)} %get-tuple-element.6.in_q, bf16[1,64,5120]{2,1,0:T(8,128)(2,1)S(1)} %get-tuple-element.7.in_k, bf16[1,64,5120]{2,1,0:T(8,128)(2,1)S(1)} %get-tuple-element.8.in_v), custom_call_target="tpu_custom_call" | custom-call | bytes 3932160 | tf_op jit(solution)/shard_map/write_out/pallas_call | solution.py:532

commit v4 on v3

--- a/solution.py
+++ b/solution.py
@@ -54,6 +54,9 @@
     upper = me >= half
     has_before, has_after = group > 0, group < groups - 1
     has_far = has_before & has_after
+    chip_at = lax.rem((group - lax.rem(group + 1, 2) * 2 + groups) // 2, 4)
+    first = (odd & (chip_at < 3)) | (even & (chip_at >= 3))
+    second = (odd & (chip_at >= 3)) | (even & (chip_at < 3))
     near = lax.rem(group, 2) * before + (1 - lax.rem(group, 2)) * after
     far = lax.rem(group, 2) * after + (1 - lax.rem(group, 2)) * before
 
@@ -131,16 +134,16 @@
         def _(part):
             pl.semaphore_signal(sem, inc=1, device_id=(far, part), device_id_type=MESH)
 
-    @pl.when(odd & has_far)
+    @pl.when(second & has_far)
     def _():
         pl.semaphore_wait(barrier, 2 * parts)
         greet_far(far_ready)
 
-    @pl.when(even | jnp.logical_not(has_far))
+    @pl.when(first | jnp.logical_not(has_far))
     def _():
         pl.semaphore_wait(barrier, parts)
 
-    @pl.when(even & has_far)
+    @pl.when(first & has_far)
     def _():
         greet_far(barrier)
 
@@ -154,7 +157,7 @@
                 g_send, g_recv.at[i], (group, peer),
             ).start()
 
-    @pl.when(even & has_far)
+    @pl.when(first & has_far)
     def _():
         pl.semaphore_wait(far_ready, parts)
 

time: 58 us -> 57.5 us (level)
  Pallas kernels: 56.7 us -> 55.7 us
    pallas_call x1, Pallas kernels: 55.4 us -> 54.4 us  [on_device(): pl.pallas_call(kernel, out_shape=(out, out, out), in_specs=[anywhere] * 8...]
where the time goes in v4:
time: 57.5 us; the launch traced here: 56.4 us
  Pallas kernels  55.7 us (97%)
  between operations  0.64 us (1%)
    pallas_call x1, Pallas kernels, on_device(): pl.pallas_call(kernel, out_shape=(out, out, out), in_specs=[anywhere] * 8...  54.4 us
    pallas_call x1, Pallas kernels, on_device(): pl.pallas_call(write_kernel, out_shape=(out, out, out), in_specs=[vmem] *...  1.3 us

profile of v4, /device:TPU:7, one launch (start us, length us, event | category | flops | bytes accessed | tf_op | source)
XLA Modules:
  0.0 56.4 jit_solution(13862833484232476290)
XLA Ops:
  0.6 54.4 %attention_backward.1 = (bf16[1,64,5120]{2,1,0:T(8,128)(2,1)S(1)}, bf16[1,64,5120]{2,1,0:T(8,128)(2,1)S(1)}, bf16[1,64,5120]{2,1,0:T(8,128)(2,1)S(1)}) custom-call(s32[32]{0:T(128)} %len_hbm.1, s32[32]{0:T(128)} %source_hbm.1, bf16[1,512,640]{2,1,0:T(8,128)(2,1)} %q_hbm.1, bf16[1,512,640]{2,1,0:T(8,128)(2,1)} %k_hbm.1, bf16[1,512,640]{2,1,0:T(8,128)(2,1)} %v_hbm.1, ...), custom_call_target="tpu_custom_call" | custom-call | flops 3355443200 | bytes 5242880 | tf_op jit(solution)/shard_map/attention_backward/pallas_call | solution.py:509
  55.1 1.3 %write_out.1 = (bf16[1,64,5120]{2,1,0:T(8,128)(2,1)}, bf16[1,64,5120]{2,1,0:T(8,128)(2,1)}, bf16[1,64,5120]{2,1,0:T(8,128)(2,1)}) custom-call(bf16[1,64,5120]{2,1,0:T(8,128)(2,1)S(1)} %get-tuple-element.6.in_q, bf16[1,64,5120]{2,1,0:T(8,128)(2,1)S(1)} %get-tuple-element.7.in_k, bf16[1,64,5120]{2,1,0:T(8,128)(2,1)S(1)} %get-tuple-element.8.in_v), custom_call_target="tpu_custom_call" | custom-call | bytes 3932160 | tf_op jit(solution)/shard_map/write_out/pallas_call | solution.py:535

commit v5 on v4

--- a/solution.py
+++ b/solution.py
@@ -280,9 +280,7 @@
             @pl.when(odd)
             def _():
                 stage[1, i] = grad_k.astype(jnp.bfloat16)
-                send_out(1, i)
                 stage[2, i] = grad_v.astype(jnp.bfloat16)
-                send_out(2, i)
 
         @pl.loop(0, heads)
         def _(i):
@@ -315,6 +313,11 @@
 
             send_out(0, i)
 
+            @pl.when(odd)
+            def _():
+                send_out(1, i)
+                send_out(2, i)
+
             @pl.when(even & (i > 0))
             def _():
                 finish_keys(i - 1)
@@ -378,7 +381,6 @@
             @pl.when(even)
             def _():
                 stage[0, i] = (grad_q * SCALE).astype(jnp.bfloat16)
-                send_out(0, i)
 
             @pl.when(odd)
             def _():
@@ -421,6 +423,10 @@
 
             send_out(1, i)
             send_out(2, i)
+
+            @pl.when(even)
+            def _():
+                send_out(0, i)
 
             @pl.when(odd & (i > 0))
             def _():

time: 57.5 us -> 57.3 us (level); the launches traced: 56.4 us -> 57.1 us
  Pallas kernels: 55.7 us -> 56.5 us
    pallas_call x1, Pallas kernels: 54.4 us -> 55.2 us  [on_device(): pl.pallas_call(kernel, out_shape=(out, out, out), in_specs=[anywhere] * 8...]
where the time goes in v5:
time: 57.3 us; the launch traced here: 57.1 us
  Pallas kernels  56.5 us (99%)
  between operations  0.64 us (1%)
    pallas_call x1, Pallas kernels, on_device(): pl.pallas_call(kernel, out_shape=(out, out, out), in_specs=[anywhere] * 8...  55.2 us
    pallas_call x1, Pallas kernels, on_device(): pl.pallas_call(write_kernel, out_shape=(out, out, out), in_specs=[vmem] *...  1.3 us

profile of v5, /device:TPU:7, one launch (start us, length us, event | category | flops | bytes accessed | tf_op | source)
XLA Modules:
  0.0 57.1 jit_solution(16867973365415483936)
XLA Ops:
  0.6 55.2 %attention_backward.1 = (bf16[1,64,5120]{2,1,0:T(8,128)(2,1)S(1)}, bf16[1,64,5120]{2,1,0:T(8,128)(2,1)S(1)}, bf16[1,64,5120]{2,1,0:T(8,128)(2,1)S(1)}) custom-call(s32[32]{0:T(128)} %len_hbm.1, s32[32]{0:T(128)} %source_hbm.1, bf16[1,512,640]{2,1,0:T(8,128)(2,1)} %q_hbm.1, bf16[1,512,640]{2,1,0:T(8,128)(2,1)} %k_hbm.1, bf16[1,512,640]{2,1,0:T(8,128)(2,1)} %v_hbm.1, ...), custom_call_target="tpu_custom_call" | custom-call | flops 3355443200 | bytes 5242880 | tf_op jit(solution)/shard_map/attention_backward/pallas_call | solution.py:515
  55.8 1.3 %write_out.1 = (bf16[1,64,5120]{2,1,0:T(8,128)(2,1)}, bf16[1,64,5120]{2,1,0:T(8,128)(2,1)}, bf16[1,64,5120]{2,1,0:T(8,128)(2,1)}) custom-call(bf16[1,64,5120]{2,1,0:T(8,128)(2,1)S(1)} %get-tuple-element.6.in_q, bf16[1,64,5120]{2,1,0:T(8,128)(2,1)S(1)} %get-tuple-element.7.in_k, bf16[1,64,5120]{2,1,0:T(8,128)(2,1)S(1)} %get-tuple-element.8.in_v), custom_call_target="tpu_custom_call" | custom-call | bytes 3932160 | tf_op jit(solution)/shard_map/write_out/pallas_call | solution.py:541
